TPU v7x, 1024 devices: a whole 4x8x16 slice. The times are simulated.
1024 devices in a mesh: owner: 16 (over y, core), split: 16 (over z), rep: 4 (over x).
Axes of the slice: x: 4, y: 8, z: 16, core: 2. Of those that a mesh axis runs over, the one named last changes fastest.
Arguments:
- embeddings: bfloat16 [196608, 1024], P(('rep', 'owner', 'split')), parts along dimension 0, may hold values from -20 to 20
- cluster: int32 [196608], P(('rep', 'owner', 'split')), parts along dimension 0, may hold values from 0 to 15, as said below
- rank: int32 [196608], P(('rep', 'owner', 'split')), parts along dimension 0, may hold values from 0 to 49151, each once
Outputs:
- best: float32 [196608], P(('rep', 'owner', 'split')), parts along dimension 0
There are 4 independent parts, one for each index of `rep`. A program takes and returns all parts, laid end to end along the dimension named above; each array names one. Nothing has to cross between parts.
Inputs may be any that keep to these rules, and one draw needn't show every extreme that they name: `cluster`: cluster c belongs to owner index c mod 16. Among the 192 rows of one device at most 18 belong to clusters of one owner index, and exactly 18 for some owner index on every device.
All inputs are finite; a program needn't handle non-finite values.
Results may differ from a plain program's by a relative error of at most 0.00048.
Values may be sent and summed in bfloat16 or wider, within the bound.
No kernel may reach another device: no remote copies, remote signals or barrier semaphores. Data moves between devices by JAX's collectives and lax.ppermute only.
A program may use at most 32 MiB of HBM per device.

v0:
```python
import jax
import jax.numpy as jnp
from jax import lax
from jax.sharding import PartitionSpec as P


def tile_scores(left, right):
    return lax.dot_general(
        left, right, (((1,), (1,)), ((), ())), preferred_element_type=jnp.float32
    )


def shards(embeddings, cluster, rank):
    rows, width = embeddings.shape
    owners = lax.axis_size("owner")
    capacity = max(2, (3 * rows + 2 * owners - 1) // (2 * owners))
    slots = owners * capacity
    wide = embeddings.astype(jnp.float32)
    unit = (wide / jnp.sqrt(jnp.sum(wide * wide, axis=1, keepdims=True) + 1e-06)).astype(
        jnp.bfloat16
    )
    target = cluster % owners
    ordinal = jnp.arange(rows, dtype=jnp.int32)
    earlier = (target[:, None] == target[None, :]) & (ordinal[:, None] > ordinal[None, :])
    position = jnp.sum(earlier.astype(jnp.int32), axis=1)
    slot_of = target * capacity + position
    placing = slot_of[:, None] == jnp.arange(slots, dtype=jnp.int32)[None, :]
    outgoing = jnp.einsum(
        "rs,rd->sd", placing.astype(jnp.bfloat16), unit, preferred_element_type=jnp.float32
    ).astype(jnp.bfloat16)
    filled = jnp.any(placing, axis=0)
    send_cluster = jnp.where(filled, jnp.sum(jnp.where(placing, cluster[:, None], 0), axis=0), -1)
    send_rank = jnp.sum(jnp.where(placing, rank[:, None], 0), axis=0)
    arrived = (
        lax.all_to_all(
            outgoing.reshape(owners, capacity, width),
            "owner",
            split_axis=0,
            concat_axis=0,
            tiled=True,
        ),
        lax.all_to_all(
            send_cluster.reshape(owners, capacity), "owner", split_axis=0, concat_axis=0, tiled=True
        ),
        lax.all_to_all(
            send_rank.reshape(owners, capacity), "owner", split_axis=0, concat_axis=0, tiled=True
        ),
    )
    keys = arrived[0].reshape(slots, width)
    key_cluster = arrived[1].reshape(slots)
    key_rank = arrived[2].reshape(slots)
    initial = jnp.full((slots,), -1.0, jnp.float32)
    scores = tile_scores(keys, lax.all_gather(keys, "split", axis=0, tiled=True))
    valid = (
        (key_cluster[:, None] == lax.all_gather(key_cluster, "split", axis=0, tiled=True)[None, :])
        & (lax.all_gather(key_rank, "split", axis=0, tiled=True)[None, :] < key_rank[:, None])
        & (key_cluster[:, None] >= 0)
    )
    result = jnp.maximum(initial, jnp.max(jnp.where(valid, scores, jnp.float32(-1.0)), axis=1))
    homeward = lax.all_to_all(
        result.reshape(owners, capacity), "owner", split_axis=0, concat_axis=0, tiled=True
    )
    return homeward.reshape(slots)[slot_of]


def solution(mesh):
    return jax.shard_map(
        shards,
        mesh=mesh,
        in_specs=(
            P(("rep", "owner", "split"), None),
            P(("rep", "owner", "split")),
            P(("rep", "owner", "split")),
        ),
        out_specs=P(("rep", "owner", "split")),
        check_vma=False,
    )
```

profile of v0, /device:TPU:6, one launch (start us, length us, event | category | flops | bytes accessed | tf_op | source)
XLA Modules:
  0.0 200.6 jit_solution(8571661233751070422)
XLA Ops:
  6.5 0.0 copy-start
  6.5 0.0 copy-start.1
  6.5 0.0 all-gather.2.cloned.1.call-start
  6.5 0.8 and_select_fusion
  7.3 0.2 convert_reduce_fusion
  7.5 0.7 compare_select_fusion
  8.2 1.2 fusion.1
  9.3 1.4 convolution_convert_fusion
  10.8 0.2 reshape.86
  11.0 29.4 %all_to_all.26 = bf16[16,18,1024]{2,1,0:T(8,128)(2,1)S(1)} all-to-all(bf16[16,18,1024]{2,1,0:T(8,128)(2,1)S(1)} %reshape.86), channel_id=1, replica_groups=mesh['owner'=16,'split'=16,'rep'=4] {'owner'}, dimensions={0} | all-to-all | bytes 1179648 | tf_op jit(solution)/shard_map/all_to_all | solution.py:35
  40.4 1.0 reshape.87
  41.4 0.0 all-gather.2.cloned.1.call-update
  41.4 0.1 fusion.5
  41.5 0.0 copy-done
  41.5 0.0 copy-done.1
  41.5 0.2 select_reduce_fusion
  41.7 0.7 select_n.39
  42.4 3.5 %all-to-all-start = ((s32[16,1,18]{2,1,0:T(1,128)}), s32[16,1,18]{2,1,0:T(1,128)S(1)}, u32[]{:S(2)}, u32[]{:S(2)}) async-start(s32[16,1,18]{2,1,0:T(1,128)} %select_n.39), calls=%async_computation | async-start | bytes 16384 | tf_op jit(solution)/shard_map/all_to_all | solution.py:42
  45.9 0.7 all_to_all.18
  46.6 6.8 %all-to-all-done = s32[16,1,18]{2,1,0:T(1,128)S(1)} async-done(((s32[16,1,18]{2,1,0:T(1,128)}), s32[16,1,18]{2,1,0:T(1,128)S(1)}, u32[]{:S(2)}, u32[]{:S(2)}) %all-to-all-start) | async-done | bytes 1184 | tf_op jit(solution)/shard_map/all_to_all | solution.py:42
  53.4 3.5 %all-to-all-start.1 = ((s32[16,1,18]{2,1,0:T(1,128)}), s32[16,1,18]{2,1,0:T(1,128)S(1)}, u32[]{:S(2)}, u32[]{:S(2)}) async-start(s32[16,1,18]{2,1,0:T(1,128)} %all_to_all.18), calls=%async_computation.1 | async-start | bytes 16384 | tf_op jit(solution)/shard_map/all_to_all | solution.py:45
  56.9 1.3 dynamic-slice
  58.8 0.5 broadcast.61
  59.3 0.7 reduce.9
  60.0 0.1 reshape.98
  60.1 4.3 %all-to-all-done.1 = s32[16,1,18]{2,1,0:T(1,128)S(1)} async-done(((s32[16,1,18]{2,1,0:T(1,128)}), s32[16,1,18]{2,1,0:T(1,128)S(1)}, u32[]{:S(2)}, u32[]{:S(2)}) %all-to-all-start.1) | async-done | bytes 1184 | tf_op jit(solution)/shard_map/all_to_all | solution.py:45
  64.4 0.7 reduce.10
  65.1 0.1 reshape.101
  65.2 0.3 dynamic-update-slice
  65.5 0.3 dynamic-update-slice.1
  65.7 69.4 %all-reduce.2 = (s32[4608]{0:T(1024)S(1)}, s32[4608]{0:T(1024)S(1)}) all-reduce(s32[4608]{0:T(1024)S(1)} %dynamic-update-slice.1, s32[4608]{0:T(1024)S(1)} %dynamic-update-slice), channel_id=1, replica_groups=mesh['owner'=16,'split'=16,'rep'=4] {'split'}, use_global_device_ids=true, to_apply=%add.1 | all-reduce | flops 9216 | bytes 73728
  135.2 32.6 %all-gather.2.cloned.1.call-done = bf16[4608,1024]{1,0:T(8,128)(2,1)} async-done(((bf16[288,1024]{1,0:T(8,128)(2,1)}), bf16[4608,1024]{1,0:T(8,128)(2,1)}) %all-gather.2.cloned.1.call-update) | async-done | bytes 9437200 | tf_op jit(solution)/shard_map/all_gather | solution.py:53
  167.7 7.5 %fusion = f32[288]{0:T(512)S(1)} fusion(bf16[288,1024]{1,0:T(8,128)(2,1)} %reshape.87, bf16[4608,1024]{1,0:T(8,128)(2,1)} %all-gather.2.cloned.1.call-done, pred[288]{0:T(512)(128)(4,1)S(1)} %broadcast_compare_fusion, s32[288]{0:T(512)S(1)} %reshape.101, s32[4608]{0:T(1024)S(1)} %get-tuple-element.7, s32[4608]{0:T(1024)S(1)} %get-tuple-element.8, ...), kind=kOutput, calls=%fused_computation.2 | convolution fusion | flops 2725871360 | bytes 10067616 | tf_op jit(solution)/shard_map/dot_general | solution.py:8
  175.2 0.7 max_broadcast_in_dim.15
  175.9 6.8 %all-to-all-start.3 = ((f32[16,1,18]{2,1,0:T(1,128)}), f32[16,1,18]{2,1,0:T(1,128)S(1)}, u32[]{:S(2)}, u32[]{:S(2)}) async-start(f32[16,1,18]{2,1,0:T(1,128)} %max_broadcast_in_dim.15), calls=%async_computation.3 | async-start | bytes 16384 | tf_op jit(solution)/shard_map/all_to_all | solution.py:60
  182.8 7.5 %all-to-all-done.3 = f32[16,1,18]{2,1,0:T(1,128)S(1)} async-done(((f32[16,1,18]{2,1,0:T(1,128)}), f32[16,1,18]{2,1,0:T(1,128)S(1)}, u32[]{:S(2)}, u32[]{:S(2)}) %all-to-all-start.3) | async-done | bytes 1184 | tf_op jit(solution)/shard_map/all_to_all | solution.py:60
  190.3 0.5 broadcast.63
  190.8 0.7 reduce.11
  191.5 0.1 reshape.88
  191.6 2.2 %gather_fusion = f32[192]{0:T(256)} fusion(f32[288]{0:T(512)S(1)} %reshape.88, s32[1024]{0:T(1024)S(1)} %pad_clamp_fusion), kind=kCustom, calls=%fused_computation | custom fusion | bytes 2304 | tf_op jit(solution)/shard_map/gather | solution.py:63
  (7 shorter events, 0.0 us)
Async XLA Ops:
  6.5 35.0 %copy-start = (s32[192]{0:T(256)S(1)}, s32[192]{0:T(256)}, u32[]{:S(2)}) copy-start(s32[192]{0:T(256)} %param.4) | copy-start | bytes 2308
  6.5 35.0 %copy-start.1 = (s32[192]{0:T(256)S(1)}, s32[192]{0:T(256)}, u32[]{:S(2)}) copy-start(s32[192]{0:T(256)} %param.5) | copy-start | bytes 2308
  6.5 161.2 %all-gather.2.cloned.1.call-start = ((), (), s32[]{:S(2)}) async-start(), calls=%async_computation.4 | async-start | bytes 10027008 | tf_op jit(solution)/shard_map/all_gather | solution.py:53
  42.4 11.0 %all-to-all-start = ((s32[16,1,18]{2,1,0:T(1,128)}), s32[16,1,18]{2,1,0:T(1,128)S(1)}, u32[]{:S(2)}, u32[]{:S(2)}) async-start(s32[16,1,18]{2,1,0:T(1,128)} %select_n.39), calls=%async_computation | async-start | bytes 16384 | tf_op jit(solution)/shard_map/all_to_all | solution.py:42
  53.4 11.0 %all-to-all-start.1 = ((s32[16,1,18]{2,1,0:T(1,128)}), s32[16,1,18]{2,1,0:T(1,128)S(1)}, u32[]{:S(2)}, u32[]{:S(2)}) async-start(s32[16,1,18]{2,1,0:T(1,128)} %all_to_all.18), calls=%async_computation.1 | async-start | bytes 16384 | tf_op jit(solution)/shard_map/all_to_all | solution.py:45
  175.9 14.4 %all-to-all-start.3 = ((f32[16,1,18]{2,1,0:T(1,128)}), f32[16,1,18]{2,1,0:T(1,128)S(1)}, u32[]{:S(2)}, u32[]{:S(2)}) async-start(f32[16,1,18]{2,1,0:T(1,128)} %max_broadcast_in_dim.15), calls=%async_computation.3 | async-start | bytes 16384 | tf_op jit(solution)/shard_map/all_to_all | solution.py:60
Sparse Core Ops, SparseCore 0:
  41.5 126.1 all-gather.1
where the time goes:
time: 202 us; the launch traced here: 201 us
  blocking collectives  98.8 us (49%)
  waiting for transfers between devices  51.3 us (25%)
  between operations  14.2 us (7%)
  starting transfers between devices  13.8 us (7%)
  matrix products  8.93 us (4%)
  local copies, waits for them, and re-layouts  8.53 us (4%)
  other arithmetic  5.1 us (3%)
    unnamed x1, blocking collectives  69.4 us
    all_gather x1, waiting for transfers between devices, shards(): lax.all_gather(keys, 'split', axis=0, tiled=True)  32.6 us
    all_to_all x1, blocking collectives, shards(): lax.all_to_all(outgoing.reshape(owners, capacity, width), 'owner', split_...  29.4 us
    all_to_all x1, waiting for transfers between devices, shards(): lax.all_to_all(result.reshape(owners, capacity), 'owner', split_axis=0, c...  7.55 us
    dot_general x1, matrix products, tile_scores(): lax.dot_general(left, right, (((1,), (1,)), ((), ())), preferred_element_...  7.49 us
    all_to_all x1, starting transfers between devices, shards(): lax.all_to_all(result.reshape(owners, capacity), 'owner', split_axis=0, c...  6.83 us
    all_to_all x1, waiting for transfers between devices, shards(): lax.all_to_all(send_cluster.reshape(owners, capacity), 'owner', split_axi...  6.82 us
    all_to_all x1, waiting for transfers between devices, shards(): lax.all_to_all(send_rank.reshape(owners, capacity), 'owner', split_axis=0...  4.31 us
  transfers between devices with their start and end apart: 4, of which 4 were waited for; matrix products, arithmetic and copies ran while one was open for 2% of the time, Pallas kernels for 0%

commit v1 on v0

v1 whole, which is shorter than its diff:
```python
import functools

import jax
import jax.numpy as jnp
from jax import lax
from jax.experimental import pallas as pl
from jax.experimental.pallas import tpu as pltpu
from jax.sharding import PartitionSpec as P

MAIN = 16
REM = 2
RANK_TILE = 8
LANES = 128
ABSENT = 256.0

NT = (((1,), (1,)), ((), ()))
NN = (((1,), (0,)), ((), ()))


def dot(left, right, dims):
    return lax.dot_general(left, right, dims, preferred_element_type=jnp.float32)


def iota(shape, dim):
    return lax.broadcasted_iota(jnp.int32, shape, dim)


def to_column(row):
    n = row.shape[1]
    return jnp.sum(jnp.where(iota((n, n), 0) == iota((n, n), 1), row, 0.0), axis=1, keepdims=True)


def to_row(column):
    n = column.shape[0]
    return jnp.sum(jnp.where(iota((n, n), 0) == iota((n, n), 1), column, 0.0), axis=0, keepdims=True)


def pack_kernel(groups, home_ref, emb_ref, cluster_ref, rank_ref, out_ref, place_ref):
    rows, width = emb_ref.shape
    pieces = width // LANES
    home = home_ref[0]
    wide = emb_ref[...].astype(jnp.float32)
    norm = jnp.sqrt(jnp.sum(wide * wide, axis=1, keepdims=True) + 1e-06)
    unit = (wide / norm).astype(jnp.bfloat16)

    target = lax.rem(cluster_ref[...], groups)
    target_column = to_column(target.astype(jnp.float32)).astype(jnp.int32)
    earlier = (target_column == target) & (iota((rows, rows), 0) < iota((rows, rows), 1))
    position = jnp.sum(earlier.astype(jnp.float32), axis=0, keepdims=True).astype(jnp.int32)
    is_main = position < MAIN
    place_ref[...] = jnp.where(
        is_main, home * MAIN + position, groups * MAIN + home * REM + position - MAIN
    )

    slot = jnp.where(is_main, target * MAIN + position, -1)
    placing = (iota((groups * MAIN, rows), 0) == slot).astype(jnp.bfloat16)
    main = dot(placing, unit, NN).astype(jnp.bfloat16)
    for k in range(pieces):
        piece = main[:, k * LANES : (k + 1) * LANES]
        out_ref[:, k * MAIN : (k + 1) * MAIN, :] = piece.reshape(groups, MAIN, LANES)

    spread = pieces * REM
    rest = jnp.zeros((groups * spread, LANES), jnp.float32)
    for k in range(pieces):
        slot = jnp.where(is_main, -1, target * spread + k * REM + position - MAIN)
        placing = (iota((groups * spread, rows), 0) == slot).astype(jnp.bfloat16)
        rest += dot(placing, unit[:, k * LANES : (k + 1) * LANES], NN)

    rank = rank_ref[...]
    high = (rank >> 8).astype(jnp.float32) - ABSENT
    low = (rank & 255).astype(jnp.float32)
    line = iota((groups * RANK_TILE, rows), 0)
    mine = line // RANK_TILE == target
    line = line % RANK_TILE
    band = home * MAIN // LANES
    lane = iota((LANES, rows), 0)
    at_main = (lane == jnp.where(is_main, lax.rem(home * MAIN, LANES) + position, -1)).astype(
        jnp.bfloat16
    )
    at_rest = (lane == jnp.where(is_main, -1, home * REM + position - MAIN)).astype(jnp.bfloat16)

    def values(first):
        value = jnp.where(line == first, high, jnp.where(line == first + 1, low, 0.0))
        return jnp.where(mine, value, 0.0).astype(jnp.bfloat16)

    tile = dot(values(2 * band), at_main, NT) + dot(values(4), at_rest, NT)
    shape = (groups * RANK_TILE, LANES)
    line, lane = iota(shape, 0) % RANK_TILE, iota(shape, 1)
    from_main = (line == 2 * band) & (lane // MAIN == lax.rem(home, LANES // MAIN))
    from_rest = (line == 4) & (lane // REM == home)
    tile += jnp.where(from_main | from_rest, ABSENT, 0.0)
    tail = jnp.concatenate(
        [rest.reshape(groups, spread, LANES), tile.reshape(groups, RANK_TILE, LANES)], axis=1
    )
    out_ref[:, pieces * MAIN :, :] = tail.astype(jnp.bfloat16)


def score_kernel(groups, pieces, targets_ref, *refs):
    counts = (2, 2, 2, 1, 2, 2)
    blocks, at = [], 0
    for count in counts:
        blocks.append(refs[at : at + count])
        at += count
    out_ref, main_ref, rest_ref, query_ref = refs[at:]
    mains, rests, spread = groups * MAIN, groups * REM, pieces * REM
    block_rows = mains + rests

    def unpack(parts, to_main, to_rest, main_at, rest_at):
        tiles, tails, row = 0.0, [], 0
        for part in parts:
            senders = part.shape[0]
            for k in range(pieces):
                to_main[pl.ds(main_at + row, senders * MAIN), k * LANES : (k + 1) * LANES] = part[
                    :, k * MAIN : (k + 1) * MAIN, :
                ].reshape(senders * MAIN, LANES)
            row += senders * MAIN
            tail = part[:, pieces * MAIN :, :].astype(jnp.float32)
            tiles = tiles + jnp.sum(tail[:, spread:, :], axis=0)
            tails.append(tail[:, :spread, :].reshape(senders * spread, LANES).astype(jnp.bfloat16))
        tail = jnp.concatenate(tails, axis=0) if len(tails) > 1 else tails[0]
        shape = (rests, groups * spread)
        line, column = iota(shape, 0), iota(shape, 1)
        for k in range(pieces):
            pick = (column == line // REM * spread + k * REM + line % REM).astype(jnp.bfloat16)
            to_rest[pl.ds(rest_at, rests), k * LANES : (k + 1) * LANES] = dot(pick, tail, NN).astype(
                jnp.bfloat16
            )
        main = [tiles[2 * g : 2 * g + 1] * 256.0 + tiles[2 * g + 1 : 2 * g + 2] for g in range(mains // LANES)]
        return jnp.concatenate(main, axis=1), (tiles[4:5] * 256.0 + tiles[5:6])[:, :rests]

    other, own = blocks[0], blocks[1:]
    main_ranks, rest_ranks = [], []
    for i, parts in enumerate(own):
        main, rest = unpack(parts, main_ref, rest_ref, i * mains, i * rests)
        main_ranks.append(main)
        rest_ranks.append(rest)
    other_main, other_rest = unpack(other, query_ref, query_ref, block_rows, block_rows + mains)
    query_ref[pl.ds(0, mains), :] = main_ref[pl.ds(0, mains), :]
    query_ref[pl.ds(mains, rests), :] = rest_ref[pl.ds(0, rests), :]
    query_ranks = [
        jnp.concatenate([to_column(main_ranks[0]), to_column(rest_ranks[0])], axis=0),
        jnp.concatenate([to_column(other_main), to_column(other_rest)], axis=0),
    ]
    rest_rank = jnp.concatenate(rest_ranks, axis=1)
    window = len(own)

    best_query = [None, None]
    best_main = [None] * window
    best_rest = None
    for q in range(2):
        query = query_ref[pl.ds(q * block_rows, block_rows), :]
        for i in range(window + 1):
            if i < window:
                key, key_rank = main_ref[pl.ds(i * mains, mains), :], main_ranks[i]
            else:
                key, key_rank = rest_ref[...], rest_rank
            scores = dot(query, key, NT)
            lower = key_rank < query_ranks[q]
            found = jnp.max(jnp.where(lower, scores, -1.0), axis=1, keepdims=True)
            best_query[q] = found if best_query[q] is None else jnp.maximum(best_query[q], found)
            if q == 0 and i == 0:
                continue
            back = jnp.where(lower, -1.0, scores)
            if q == 0 and i == window:
                back = jnp.where(iota(back.shape, 1) < rests, -1.0, back)
            found = jnp.max(back, axis=0, keepdims=True)
            if i < window:
                best_main[i] = found if best_main[i] is None else jnp.maximum(best_main[i], found)
            else:
                best_rest = found if best_rest is None else jnp.maximum(best_rest, found)

    queries = [jnp.concatenate([to_row(b[:mains]), to_row(b[mains:])], axis=1) for b in best_query]
    lines = [jnp.concatenate([best_main[i], best_rest[:, i * rests : (i + 1) * rests]], axis=1) for i in range(window)]
    lines[0] = jnp.maximum(lines[0], queries[0])
    lines.append(queries[1])
    targets = out_ref.shape[0]
    line = iota((targets, block_rows), 0)
    out = jnp.full((targets, block_rows), -1.0, jnp.float32)
    for i, value in enumerate(lines):
        out = jnp.where(line == targets_ref[i], value, out)
    pad = out_ref.shape[2] - block_rows
    out = jnp.concatenate([out, jnp.full((targets, pad), -1.0, jnp.float32)], axis=1)
    out_ref[...] = out.reshape(out_ref.shape)


def pick_kernel(groups, arrived_ref, cluster_ref, place_ref, out_ref):
    arrived = arrived_ref[...].reshape(groups, arrived_ref.shape[2])
    rows = place_ref.shape[1]
    place = (iota((arrived.shape[1], rows), 0) == place_ref[...]).astype(jnp.bfloat16)
    found = jnp.zeros((groups, rows), jnp.float32)
    left = arrived
    for _ in range(3):
        term = left.astype(jnp.bfloat16)
        found += dot(term, place, NN)
        left = left - term.astype(jnp.float32)
    target = lax.rem(cluster_ref[...], groups)
    mine = iota((groups, rows), 0) == target
    out_ref[...] = jnp.sum(jnp.where(mine, found, 0.0), axis=0, keepdims=True)


def shards(embeddings, cluster, rank):
    rows, width = embeddings.shape
    owners, groups = lax.axis_size("owner"), lax.axis_size("split")
    pieces = width // LANES
    depth = pieces * (MAIN + REM) + RANK_TILE
    block_rows = groups * (MAIN + REM)
    padded = -(-block_rows // LANES) * LANES
    owner = lax.axis_index("owner").astype(jnp.int32)
    home = lax.axis_index("split").astype(jnp.int32)
    cluster, rank = cluster.reshape(1, rows), rank.reshape(1, rows)
    smem = pl.BlockSpec(memory_space=pltpu.SMEM)
    vmem = pl.BlockSpec(memory_space=pltpu.VMEM)
    params = pltpu.CompilerParams(vmem_limit_bytes=40 * 1024 * 1024)

    packed, place = pl.pallas_call(
        functools.partial(pack_kernel, groups),
        out_shape=(
            jax.ShapeDtypeStruct((groups, depth, LANES), jnp.bfloat16),
            jax.ShapeDtypeStruct((1, rows), jnp.int32),
        ),
        in_specs=[smem, vmem, vmem, vmem],
        out_specs=(vmem, vmem),
        compiler_params=params,
        name="pack",
    )(home.reshape(1), embeddings, cluster, rank)

    block = lax.all_to_all(packed, "split", split_axis=0, concat_axis=0, tiled=True)

    def shift(value, chips):
        return lax.ppermute(value, "owner", [(o, (o + 2 * chips) % owners) for o in range(owners)])

    def swap(value):
        return lax.ppermute(value, "owner", [(o, o ^ 1) for o in range(owners)])

    halves = (block[: groups // 2], block[groups // 2 :])
    back1 = [shift(h, 1) for h in halves]
    ahead1 = [shift(h, -1) for h in halves]
    back2 = [shift(h, 1) for h in back1]
    ahead2 = [shift(h, -1) for h in ahead1]
    other2 = [swap(h) for h in back2]

    chip, core = owner // 2, owner % 2
    chips = owners // 2
    targets = [lax.rem(chip + chips + d, chips) * 2 + core for d in (-2, -1, 0, 1, 2)]
    targets.append(lax.rem(chip + chips - 2, chips) * 2 + 1 - core)
    window = 5
    best = pl.pallas_call(
        functools.partial(score_kernel, groups, pieces),
        out_shape=jax.ShapeDtypeStruct((owners, 1, padded), jnp.float32),
        in_specs=[smem] + [vmem] * 11,
        out_specs=vmem,
        scratch_shapes=[
            pltpu.VMEM((window * groups * MAIN, width), jnp.bfloat16),
            pltpu.VMEM((window * groups * REM, width), jnp.bfloat16),
            pltpu.VMEM((2 * block_rows, width), jnp.bfloat16),
        ],
        compiler_params=params,
        name="score",
    )(jnp.stack(targets), *other2, *back2, *back1, block, *ahead1, *ahead2)

    best = lax.all_to_all(best, "owner", split_axis=0, concat_axis=0, tiled=True)
    best = jnp.broadcast_to(jnp.max(best, axis=0, keepdims=True), (groups, 1, padded))
    arrived = lax.all_to_all(best, "split", split_axis=0, concat_axis=0, tiled=True)

    result = pl.pallas_call(
        functools.partial(pick_kernel, groups),
        out_shape=jax.ShapeDtypeStruct((1, rows), jnp.float32),
        in_specs=[vmem, vmem, vmem],
        out_specs=vmem,
        compiler_params=params,
        name="pick",
    )(arrived, cluster, place)
    return result.reshape(rows)


def solution(mesh):
    return jax.shard_map(
        shards,
        mesh=mesh,
        in_specs=(
            P(("rep", "owner", "split"), None),
            P(("rep", "owner", "split")),
            P(("rep", "owner", "split")),
        ),
        out_specs=P(("rep", "owner", "split")),
        check_vma=False,
    )
```

time: 202 us -> 132 us (0.65)
  waiting for transfers between devices: 51.3 us -> 3.41 us
  starting transfers between devices: 13.8 us -> 31.2 us
  between operations: 14.2 us -> 0.2 us
  blocking collectives: 98.8 us -> 89.4 us
  matrix products: 8.93 us -> 0 us
  local copies, waits for them, and re-layouts: 8.53 us -> 1.83 us
  Pallas kernels: 0 us -> 5.5 us
  other arithmetic: 5.1 us -> 0.04 us
    unnamed x1 -> x0, blocking collectives: 69.4 us -> none
    all_to_all x1 -> x3, blocking collectives: 29.4 us -> 89.4 us  [the longest x1 54.1 us: shards(): lax.all_to_all(packed, 'split', split_axis=0, concat_axis=0, tiled=True)]
    all_gather x1 -> x0, waiting for transfers between devices: 32.6 us -> none  [shards(): lax.all_gather(keys, 'split', axis=0, tiled=True)]
    ppermute x0 -> x10, starting transfers between devices: none -> 31.2 us  [the longest x8 26.8 us: shift(): lax.ppermute(value, 'owner', [(o, (o + 2 * chips) % owners) for o in rang...]
    all_to_all x3 -> x0, waiting for transfers between devices: 18.7 us -> none  [the longest x1 7.55 us: shards(): lax.all_to_all(result.reshape(owners, capacity), 'owner', split_axis=0, c...]
    all_to_all x3 -> x0, starting transfers between devices: 13.8 us -> none  [the longest x1 6.83 us: shards(): lax.all_to_all(result.reshape(owners, capacity), 'owner', split_axis=0, c...]
    dot_general x2 -> x0, matrix products: 8.93 us -> none  [the longest x1 7.49 us: tile_scores(): lax.dot_general(left, right, (((1,), (1,)), ((), ())), preferred_element_...]
    pallas_call x0 -> x3, Pallas kernels: none -> 5.5 us  [the longest x1 3.81 us: shards(): pl.pallas_call(functools.partial(score_kernel, groups, pieces), out_shape...]
  transfers between devices with their start and end apart: 4 -> 10, of which waited for: 4 -> 3; matrix products, arithmetic and copies ran while one was open for 2% -> 0% of each run, Pallas kernels for 0% -> 0%
where the time goes in v1:
time: 132 us
  blocking collectives  89.4 us (68%)
  starting transfers between devices  31.2 us (24%)
  Pallas kernels  5.5 us (4%)
  waiting for transfers between devices  3.41 us (3%)
  local copies, waits for them, and re-layouts  1.83 us (1%)
    all_to_all x1, blocking collectives, shards(): lax.all_to_all(packed, 'split', split_axis=0, concat_axis=0, tiled=True)  54.1 us
    ppermute x8, starting transfers between devices, shift(): lax.ppermute(value, 'owner', [(o, (o + 2 * chips) % owners) for o in rang...  26.8 us
    all_to_all x1, blocking collectives, shards(): lax.all_to_all(best, 'split', split_axis=0, concat_axis=0, tiled=True)  21.3 us
    all_to_all x1, blocking collectives, shards(): lax.all_to_all(best, 'owner', split_axis=0, concat_axis=0, tiled=True)  13.9 us
    ppermute x2, starting transfers between devices, swap(): return lax.ppermute(value, 'owner', [(o, o ^ 1) for o in range(owners)])  4.33 us
    pallas_call x1, Pallas kernels, shards(): pl.pallas_call(functools.partial(score_kernel, groups, pieces), out_shape...  3.81 us
    ppermute x8, waiting for transfers between devices, shift(): lax.ppermute(value, 'owner', [(o, (o + 2 * chips) % owners) for o in rang...  3.4 us
  transfers between devices with their start and end apart: 10, of which 3 were waited for; matrix products, arithmetic and copies ran while one was open for 0% of the time, Pallas kernels for 0%

profile of v1, /device:TPU:6, one launch (start us, length us, event | category | flops | bytes accessed | tf_op | source)
XLA Modules:
  0.0 131.5 jit_solution(9388911441803716765)
XLA Ops:
  0.0 0.0 copy-start.2
  0.0 0.0 copy-start.1
  0.0 0.7 copy-done.2
  0.7 0.0 copy-done.1
  0.7 0.0 copy-start
  0.7 1.0 copy-done
  1.7 0.8 pack.1
  2.5 54.1 %all_to_all.15.refs_6_ = bf16[16,152,128]{2,1,0:T(8,128)(2,1)S(1)} all-to-all(bf16[16,152,128]{2,1,0:T(8,128)(2,1)S(1)} %get-tuple-element.7), channel_id=1, replica_groups=mesh['owner'=16,'split'=16,'rep'=4] {'split'}, dimensions={0} | all-to-all | bytes 1245184 | tf_op jit(solution)/shard_map/all_to_all | solution.py:227
  56.7 3.5 %collective-permute-start.3 = (bf16[8,152,128]{2,1,0:T(8,128)(2,1)S(1)}, bf16[8,152,128]{2,1,0:T(8,128)(2,1)S(1)}, u32[]{:S(2)}, u32[]{:S(2)}) collective-permute-start(bf16[8,152,128]{2,1,0:T(8,128)(2,1)S(1)} %get-tuple-element.9), channel_id=1, source_target_pairs={{0,128},{64,192},{128,256},{192,320},{256,384},{320,448},{384,512}... | collective-permute-start | bytes 933896 | tf_op jit(solution)/shard_map/ppermute | solution.py:230
  60.2 3.5 %collective-permute-start = (bf16[8,152,128]{2,1,0:T(8,128)(2,1)S(1)}, bf16[8,152,128]{2,1,0:T(8,128)(2,1)S(1)}, u32[]{:S(2)}, u32[]{:S(2)}) collective-permute-start(bf16[8,152,128]{2,1,0:T(8,128)(2,1)S(1)} %get-tuple-element.10), channel_id=1, source_target_pairs={{0,128},{64,192},{128,256},{192,320},{256,384},{320,448},{384,512}... | collective-permute-start | bytes 933896 | tf_op jit(solution)/shard_map/ppermute | solution.py:230
  63.7 3.6 %collective-permute-start.7 = (bf16[8,152,128]{2,1,0:T(8,128)(2,1)S(1)}, bf16[8,152,128]{2,1,0:T(8,128)(2,1)S(1)}, u32[]{:S(2)}, u32[]{:S(2)}) collective-permute-start(bf16[8,152,128]{2,1,0:T(8,128)(2,1)S(1)} %get-tuple-element.9), channel_id=1, source_target_pairs={{0,896},{64,960},{128,0},{192,64},{256,128},{320,192},{384,256},{4... | collective-permute-start | bytes 933896 | tf_op jit(solution)/shard_map/ppermute | solution.py:230
  67.2 2.6 %collective-permute-start.6 = (bf16[8,152,128]{2,1,0:T(8,128)(2,1)S(1)}, bf16[8,152,128]{2,1,0:T(8,128)(2,1)S(1)}, u32[]{:S(2)}, u32[]{:S(2)}) collective-permute-start(bf16[8,152,128]{2,1,0:T(8,128)(2,1)S(1)} %get-tuple-element.10), channel_id=1, source_target_pairs={{0,896},{64,960},{128,0},{192,64},{256,128},{320,192},{384,256},{4... | collective-permute-start | bytes 933896 | tf_op jit(solution)/shard_map/ppermute | solution.py:230
  69.8 0.3 collective-permute-done.3.refs_5_
  70.1 3.0 %collective-permute-start.4 = (bf16[8,152,128]{2,1,0:T(8,128)(2,1)S(1)}, bf16[8,152,128]{2,1,0:T(8,128)(2,1)S(1)}, u32[]{:S(2)}, u32[]{:S(2)}) collective-permute-start(bf16[8,152,128]{2,1,0:T(8,128)(2,1)S(1)} %collective-permute-done.3.refs_5_), channel_id=1, source_target_pairs={{0,128},{64,192},{128,256},{192,320},{256,384},{320,448},{384,512}... | collective-permute-start | bytes 933896 | tf_op jit(solution)/shard_map/ppermute | solution.py:230
  73.1 1.8 %collective-permute-done.refs_4_ = bf16[8,152,128]{2,1,0:T(8,128)(2,1)S(1)} collective-permute-done((bf16[8,152,128]{2,1,0:T(8,128)(2,1)S(1)}, bf16[8,152,128]{2,1,0:T(8,128)(2,1)S(1)}, u32[]{:S(2)}, u32[]{:S(2)}) %collective-permute-start) | collective-permute-done | bytes 311328 | tf_op jit(solution)/shard_map/ppermute | solution.py:230
  74.9 1.9 %collective-permute-start.1 = (bf16[8,152,128]{2,1,0:T(8,128)(2,1)S(1)}, bf16[8,152,128]{2,1,0:T(8,128)(2,1)S(1)}, u32[]{:S(2)}, u32[]{:S(2)}) collective-permute-start(bf16[8,152,128]{2,1,0:T(8,128)(2,1)S(1)} %collective-permute-done.refs_4_), channel_id=1, source_target_pairs={{0,128},{64,192},{128,256},{192,320},{256,384},{320,448},{384,512}... | collective-permute-start | bytes 933896 | tf_op jit(solution)/shard_map/ppermute | solution.py:230
  76.8 0.0 collective-permute-done.7.refs_8_
  76.8 5.1 %collective-permute-start.9 = (bf16[8,152,128]{2,1,0:T(8,128)(2,1)S(1)}, bf16[8,152,128]{2,1,0:T(8,128)(2,1)S(1)}, u32[]{:S(2)}, u32[]{:S(2)}) collective-permute-start(bf16[8,152,128]{2,1,0:T(8,128)(2,1)S(1)} %collective-permute-done.7.refs_8_), channel_id=1, source_target_pairs={{0,896},{64,960},{128,0},{192,64},{256,128},{320,192},{384,256},{4... | collective-permute-start | bytes 933896 | tf_op jit(solution)/shard_map/ppermute | solution.py:230
  82.0 0.0 collective-permute-done.6.refs_7_
  82.0 3.6 %collective-permute-start.8 = (bf16[8,152,128]{2,1,0:T(8,128)(2,1)S(1)}, bf16[8,152,128]{2,1,0:T(8,128)(2,1)S(1)}, u32[]{:S(2)}, u32[]{:S(2)}) collective-permute-start(bf16[8,152,128]{2,1,0:T(8,128)(2,1)S(1)} %collective-permute-done.6.refs_7_), channel_id=1, source_target_pairs={{0,896},{64,960},{128,0},{192,64},{256,128},{320,192},{384,256},{4... | collective-permute-start | bytes 933896 | tf_op jit(solution)/shard_map/ppermute | solution.py:230
  85.6 0.0 collective-permute-done.4.refs_3_
  85.6 1.9 %collective-permute-start.5 = (bf16[8,152,128]{2,1,0:T(8,128)(2,1)S(1)}, bf16[8,152,128]{2,1,0:T(8,128)(2,1)S(1)}, u32[]{:S(2)}, u32[]{:S(2)}) collective-permute-start(bf16[8,152,128]{2,1,0:T(8,128)(2,1)S(1)} %collective-permute-done.4.refs_3_), channel_id=1, source_target_pairs={{0,64},{64,0},{128,192},{192,128},{256,320},{320,256},{384,448},{4... | collective-permute-start | bytes 933896 | tf_op jit(solution)/shard_map/ppermute | solution.py:233
  87.6 0.0 collective-permute-done.1.refs_2_
  87.6 2.4 %collective-permute-start.2 = (bf16[8,152,128]{2,1,0:T(8,128)(2,1)S(1)}, bf16[8,152,128]{2,1,0:T(8,128)(2,1)}, u32[]{:S(2)}, u32[]{:S(2)}) collective-permute-start(bf16[8,152,128]{2,1,0:T(8,128)(2,1)S(1)} %collective-permute-done.1.refs_2_), channel_id=1, source_target_pairs={{0,64},{64,0},{128,192},{192,128},{256,320},{320,256},{384,448},{4... | collective-permute-start | bytes 933896 | tf_op jit(solution)/shard_map/ppermute | solution.py:233
  90.0 0.1 stack.27.targets_ref
  90.1 0.0 collective-permute-done.9.refs_10_
  90.1 1.4 %collective-permute-done.8.refs_9_ = bf16[8,152,128]{2,1,0:T(8,128)(2,1)S(1)} collective-permute-done((bf16[8,152,128]{2,1,0:T(8,128)(2,1)S(1)}, bf16[8,152,128]{2,1,0:T(8,128)(2,1)S(1)}, u32[]{:S(2)}, u32[]{:S(2)}) %collective-permute-start.8) | collective-permute-done | bytes 311328 | tf_op jit(solution)/shard_map/ppermute | solution.py:230
  91.5 0.0 collective-permute-done.5.refs_1_
  91.5 0.0 collective-permute-done.2.refs_0_
  91.5 3.8 %score.1 = f32[16,1,384]{2,1,0:T(1,128)S(1)} custom-call(s32[6]{0:T(128)S(1)} %stack.27.targets_ref, bf16[8,152,128]{2,1,0:T(8,128)(2,1)} %collective-permute-done.2.refs_0_, bf16[8,152,128]{2,1,0:T(8,128)(2,1)S(1)} %collective-permute-done.5.refs_1_, bf16[8,152,128]{2,1,0:T(8,128)(2,1)S(1)} %collective-permute-done.1.refs_2_, ...), custom_call_target="tpu_custom_call" | custom-call | tf_op jit(solution)/shard_map/score/pallas_call | solution.py:247
  95.3 13.9 %all_to_all.16 = f32[16,1,384]{2,1,0:T(1,128)S(1)} all-to-all(f32[16,1,384]{2,1,0:T(1,128)S(1)} %score.1), channel_id=1, replica_groups=mesh['owner'=16,'split'=16,'rep'=4] {'owner'}, dimensions={0} | all-to-all | bytes 49152 | tf_op jit(solution)/shard_map/all_to_all | solution.py:261
  109.3 21.3 %all_to_all.17.arrived_ref = f32[16,1,384]{2,1,0:T(1,128)S(1)} all-to-all(f32[16,1,384]{2,1,0:T(1,128)S(1)} %broadcast_in_dim.2), channel_id=1, replica_groups=mesh['owner'=16,'split'=16,'rep'=4] {'split'}, dimensions={0} | all-to-all | bytes 49152 | tf_op jit(solution)/shard_map/all_to_all | solution.py:263
  130.6 0.9 pick.1
  (3 shorter events, 0.1 us)
Async XLA Ops:
  0.0 0.7 copy-start.2
  0.0 0.7 copy-start.1
  0.7 1.0 copy-start
  56.7 13.4 %collective-permute-start.3 = (bf16[8,152,128]{2,1,0:T(8,128)(2,1)S(1)}, bf16[8,152,128]{2,1,0:T(8,128)(2,1)S(1)}, u32[]{:S(2)}, u32[]{:S(2)}) collective-permute-start(bf16[8,152,128]{2,1,0:T(8,128)(2,1)S(1)} %get-tuple-element.9), channel_id=1, source_target_pairs={{0,128},{64,192},{128,256},{192,320},{256,384},{320,448},{384,512}... | collective-permute-start | bytes 933896 | tf_op jit(solution)/shard_map/ppermute | solution.py:230
  60.2 14.7 %collective-permute-start = (bf16[8,152,128]{2,1,0:T(8,128)(2,1)S(1)}, bf16[8,152,128]{2,1,0:T(8,128)(2,1)S(1)}, u32[]{:S(2)}, u32[]{:S(2)}) collective-permute-start(bf16[8,152,128]{2,1,0:T(8,128)(2,1)S(1)} %get-tuple-element.10), channel_id=1, source_target_pairs={{0,128},{64,192},{128,256},{192,320},{256,384},{320,448},{384,512}... | collective-permute-start | bytes 933896 | tf_op jit(solution)/shard_map/ppermute | solution.py:230
  63.7 13.1 %collective-permute-start.7 = (bf16[8,152,128]{2,1,0:T(8,128)(2,1)S(1)}, bf16[8,152,128]{2,1,0:T(8,128)(2,1)S(1)}, u32[]{:S(2)}, u32[]{:S(2)}) collective-permute-start(bf16[8,152,128]{2,1,0:T(8,128)(2,1)S(1)} %get-tuple-element.9), channel_id=1, source_target_pairs={{0,896},{64,960},{128,0},{192,64},{256,128},{320,192},{384,256},{4... | collective-permute-start | bytes 933896 | tf_op jit(solution)/shard_map/ppermute | solution.py:230
  67.2 14.7 %collective-permute-start.6 = (bf16[8,152,128]{2,1,0:T(8,128)(2,1)S(1)}, bf16[8,152,128]{2,1,0:T(8,128)(2,1)S(1)}, u32[]{:S(2)}, u32[]{:S(2)}) collective-permute-start(bf16[8,152,128]{2,1,0:T(8,128)(2,1)S(1)} %get-tuple-element.10), channel_id=1, source_target_pairs={{0,896},{64,960},{128,0},{192,64},{256,128},{320,192},{384,256},{4... | collective-permute-start | bytes 933896 | tf_op jit(solution)/shard_map/ppermute | solution.py:230
  70.1 15.5 %collective-permute-start.4 = (bf16[8,152,128]{2,1,0:T(8,128)(2,1)S(1)}, bf16[8,152,128]{2,1,0:T(8,128)(2,1)S(1)}, u32[]{:S(2)}, u32[]{:S(2)}) collective-permute-start(bf16[8,152,128]{2,1,0:T(8,128)(2,1)S(1)} %collective-permute-done.3.refs_5_), channel_id=1, source_target_pairs={{0,128},{64,192},{128,256},{192,320},{256,384},{320,448},{384,512}... | collective-permute-start | bytes 933896 | tf_op jit(solution)/shard_map/ppermute | solution.py:230
  74.9 12.7 %collective-permute-start.1 = (bf16[8,152,128]{2,1,0:T(8,128)(2,1)S(1)}, bf16[8,152,128]{2,1,0:T(8,128)(2,1)S(1)}, u32[]{:S(2)}, u32[]{:S(2)}) collective-permute-start(bf16[8,152,128]{2,1,0:T(8,128)(2,1)S(1)} %collective-permute-done.refs_4_), channel_id=1, source_target_pairs={{0,128},{64,192},{128,256},{192,320},{256,384},{320,448},{384,512}... | collective-permute-start | bytes 933896 | tf_op jit(solution)/shard_map/ppermute | solution.py:230
  76.8 13.3 %collective-permute-start.9 = (bf16[8,152,128]{2,1,0:T(8,128)(2,1)S(1)}, bf16[8,152,128]{2,1,0:T(8,128)(2,1)S(1)}, u32[]{:S(2)}, u32[]{:S(2)}) collective-permute-start(bf16[8,152,128]{2,1,0:T(8,128)(2,1)S(1)} %collective-permute-done.7.refs_8_), channel_id=1, source_target_pairs={{0,896},{64,960},{128,0},{192,64},{256,128},{320,192},{384,256},{4... | collective-permute-start | bytes 933896 | tf_op jit(solution)/shard_map/ppermute | solution.py:230
  82.0 9.5 %collective-permute-start.8 = (bf16[8,152,128]{2,1,0:T(8,128)(2,1)S(1)}, bf16[8,152,128]{2,1,0:T(8,128)(2,1)S(1)}, u32[]{:S(2)}, u32[]{:S(2)}) collective-permute-start(bf16[8,152,128]{2,1,0:T(8,128)(2,1)S(1)} %collective-permute-done.6.refs_7_), channel_id=1, source_target_pairs={{0,896},{64,960},{128,0},{192,64},{256,128},{320,192},{384,256},{4... | collective-permute-start | bytes 933896 | tf_op jit(solution)/shard_map/ppermute | solution.py:230
  85.6 5.9 %collective-permute-start.5 = (bf16[8,152,128]{2,1,0:T(8,128)(2,1)S(1)}, bf16[8,152,128]{2,1,0:T(8,128)(2,1)S(1)}, u32[]{:S(2)}, u32[]{:S(2)}) collective-permute-start(bf16[8,152,128]{2,1,0:T(8,128)(2,1)S(1)} %collective-permute-done.4.refs_3_), channel_id=1, source_target_pairs={{0,64},{64,0},{128,192},{192,128},{256,320},{320,256},{384,448},{4... | collective-permute-start | bytes 933896 | tf_op jit(solution)/shard_map/ppermute | solution.py:233
  87.6 3.9 %collective-permute-start.2 = (bf16[8,152,128]{2,1,0:T(8,128)(2,1)S(1)}, bf16[8,152,128]{2,1,0:T(8,128)(2,1)}, u32[]{:S(2)}, u32[]{:S(2)}) collective-permute-start(bf16[8,152,128]{2,1,0:T(8,128)(2,1)S(1)} %collective-permute-done.1.refs_2_), channel_id=1, source_target_pairs={{0,64},{64,0},{128,192},{192,128},{256,320},{320,256},{384,448},{4... | collective-permute-start | bytes 933896 | tf_op jit(solution)/shard_map/ppermute | solution.py:233
